TPU v7x, 32 devices: a whole 2x2x4 slice. The times are simulated.
32 devices in a mesh: cfg: 2 (over x), seq: 8 (over z, core), wgt: 2 (over y).
Axes of the slice: x: 2, y: 2, z: 4, core: 2. Of those that a mesh axis runs over, the one named last changes fastest.
Arguments:
- latent: float32 [1024, 4, 64], P(('seq', 'wgt'), 'cfg'), may hold values from -6 to 6
- img_hidden: bfloat16 [2, 1024, 4, 2432], P('cfg', 'seq'), may hold values from -5 to 5
- txt_hidden: bfloat16 [2, 512, 2432], P('cfg', 'seq'), may hold values from -6 to 6
- segments: int32 [2, 512], P('cfg', 'seq'), may hold values from 0 to 3, never falling along the last dimension, each value on 1 to 154 neighbouring positions
- timesteps: int32 [4], replicated, may hold values from 0 to 27
- modulation: float32 [2, 4, 10, 2432], P('cfg'), may hold values from -3 to 3
- qk_gain: float32 [2, 64], replicated, may hold values from 1.5 to 8
- qkv_weight: bfloat16 [3, 2432, 1536], P(None, 'seq', 'wgt'), may hold values from -0.08111071 to 0.08111071, as said below
- text_weight: bfloat16 [2, 2432, 1536], P(None, 'seq', 'wgt'), may hold values from -0.125 to 0.125
- out_weight: bfloat16 [1536, 2432], P('wgt', 'seq'), may hold values from -0.15625 to 0.15625
- expand_weight: bfloat16 [2432, 5632], P('seq', 'wgt'), may hold values from -0.125 to 0.125
- contract_weight: bfloat16 [5632, 2432], P('wgt', 'seq'), may hold values from -0.078125 to 0.078125
- final_weight: bfloat16 [2432, 64], replicated, may hold values from -0.0625 to 0.0625
Outputs:
- velocity: float32 [1024, 4, 64], P(('seq', 'wgt'), 'cfg')
- next_latent: float32 [1024, 4, 64], P(('seq', 'wgt'), 'cfg')
Inputs may be any that keep to these rules, and one draw needn't show every extreme that they name: `segments`: along each row the segment never falls, and each request has 1 to 154 positions. `qkv_weight`: entries are of order 2432 ** -0.5.
All inputs are finite; a program needn't handle non-finite values.
Results may differ from a plain program's by a relative error of at most 0.012.
The roundings to bfloat16 on the way count: a program that leaves them out, or rounds other values in their place, can miss the bound.
Values may be sent and summed in bfloat16 or wider, within the bound.
A program may use at most 128 MiB of HBM per device.

v0:
```python
import jax
import jax.numpy as jnp
from jax import lax
from jax.sharding import PartitionSpec as P

STEPS = 28


guidance_scale = 3.5
flow_shift = 3.0
eps_norm = 1e-06
masked_score = -1e30


def from_partner(value, axis, bit):
    mask = 2**bit
    pairs = [(source, source ^ mask) for source in range(lax.axis_size(axis))]
    return lax.ppermute(value, axis, pairs)


def layer_norm(values):
    center = jnp.mean(values, axis=-1, keepdims=True)
    centred = values - center
    spread = jnp.mean(centred * centred, axis=-1, keepdims=True)
    return centred * lax.rsqrt(spread + eps_norm)


def head_norm(values, gain_row):
    power = jnp.mean(values * values, axis=-1, keepdims=True)
    return values * lax.rsqrt(power + eps_norm) * gain_row


def sigma_of(index_row):
    time_left = 1.0 - index_row.astype(jnp.float32) / STEPS
    return flow_shift * time_left / (1.0 + (flow_shift - 1.0) * time_left)


def body(
    latent,
    img_hidden,
    txt_hidden,
    segments,
    timesteps,
    modulation,
    qk_gain,
    qkv_weight,
    text_weight,
    out_weight,
    expand_weight,
    contract_weight,
    final_weight,
):
    tokens_here = img_hidden.shape[1]
    requests = img_hidden.shape[2]
    feat_width = img_hidden.shape[3]
    head_size = qk_gain.shape[1]
    local_cols = qkv_weight.shape[2]
    heads_here = local_cols // head_size
    text_here = txt_hidden.shape[1]
    modulate = modulation[0]
    hidden = img_hidden[0].astype(jnp.float32)
    image_normed = (layer_norm(hidden) * (1.0 + modulate[:, 1]) + modulate[:, 0]).astype(
        jnp.bfloat16
    )
    row_count = tokens_here * requests
    token_rows = image_normed.reshape(row_count, feat_width)
    segment_row = segments[0]
    one_hot = (segment_row[:, None] == jnp.arange(requests, dtype=jnp.int32)[None, :]).astype(
        jnp.float32
    )
    text_mod = jnp.einsum("tr,rkd->tkd", one_hot, modulate[:, 3:5], precision=lax.Precision.HIGHEST)
    text_normed = (
        layer_norm(txt_hidden[0].astype(jnp.float32)) * (1.0 + text_mod[:, 1]) + text_mod[:, 0]
    ).astype(jnp.bfloat16)
    all_weights = jnp.concatenate([qkv_weight, text_weight], axis=0)
    out_full, contract_full = (
        lax.all_gather(out_weight, "seq", axis=1, tiled=True),
        lax.all_gather(contract_weight, "seq", axis=1, tiled=True),
    )
    piece = lax.all_gather(all_weights, "seq", axis=1, tiled=True)
    image_term = jnp.einsum(
        "rd,kdc->rkc", token_rows, piece[:3], preferred_element_type=jnp.float32
    )
    text_term = jnp.einsum(
        "rd,kdc->rkc", text_normed, piece[3:], preferred_element_type=jnp.float32
    )
    queries = head_norm(
        image_term[:, 0].reshape(tokens_here, requests, heads_here, head_size), qk_gain[0]
    ).astype(jnp.bfloat16)
    keys_img = head_norm(
        image_term[:, 1].reshape(tokens_here, requests, heads_here, head_size), qk_gain[1]
    ).astype(jnp.bfloat16)
    values_img = image_term[:, 2].reshape(tokens_here, requests, local_cols).astype(jnp.bfloat16)
    keys_txt = head_norm(
        text_term[:, 0].reshape(text_here, heads_here, head_size), qk_gain[1]
    ).astype(jnp.bfloat16)
    values_txt = text_term[:, 1].astype(jnp.bfloat16)
    image_pair = jnp.stack(
        [keys_img.reshape(tokens_here, requests, local_cols), values_img], axis=2
    )
    text_pair = jnp.stack([keys_txt.reshape(text_here, local_cols), values_txt], axis=1)
    text_owner = segment_row.astype(jnp.float32).astype(jnp.bfloat16)
    scale_factor = head_size ** (-0.5)
    request_ids = jnp.arange(requests, dtype=jnp.float32)
    running_max = jnp.full((requests, heads_here, tokens_here), masked_score, jnp.float32)
    image_piece = lax.all_gather(image_pair, "seq", axis=0, tiled=True)
    text_piece = lax.all_gather(text_pair, "seq", axis=0, tiled=True)
    owner_piece = lax.all_gather(text_owner, "seq", axis=0, tiled=True)
    piece_keys = image_piece[:, :, 0].reshape(-1, requests, heads_here, head_size)
    piece_values = image_piece[:, :, 1].reshape(-1, requests, heads_here, head_size)
    text_keys = text_piece[:, 0].reshape(-1, heads_here, head_size)
    text_values = text_piece[:, 1].reshape(-1, heads_here, head_size)
    image_scores = (
        jnp.einsum("qrhd,krhd->rhqk", queries, piece_keys, preferred_element_type=jnp.float32)
        * scale_factor
    )
    text_scores = (
        jnp.einsum("qrhd,khd->rhqk", queries, text_keys, preferred_element_type=jnp.float32)
        * scale_factor
    )
    allowed = owner_piece.astype(jnp.float32)[None, :] == request_ids[:, None]
    text_scores = jnp.where(allowed[:, None, None, :], text_scores, masked_score)
    block_max = jnp.maximum(jnp.max(image_scores, axis=-1), jnp.max(text_scores, axis=-1))
    new_max = jnp.maximum(running_max, block_max)
    image_weights = jnp.exp(image_scores - new_max[..., None])
    text_weights = jnp.exp(text_scores - new_max[..., None])
    new_sum = jnp.sum(image_weights, axis=-1) + jnp.sum(text_weights, axis=-1)
    new_acc = jnp.einsum(
        "rhqk,krhd->rhqd",
        image_weights.astype(jnp.bfloat16),
        piece_values,
        preferred_element_type=jnp.float32,
    )
    new_acc = new_acc + jnp.einsum(
        "rhqk,khd->rhqd",
        text_weights.astype(jnp.bfloat16),
        text_values,
        preferred_element_type=jnp.float32,
    )
    attended = new_acc / new_sum[..., None]
    attended = (
        jnp.transpose(attended, (2, 0, 1, 3)).reshape(row_count, local_cols).astype(jnp.bfloat16)
    )
    share_rows = row_count // lax.axis_size("wgt")
    piece_rows = attended
    mixed = lax.psum_scatter(
        jnp.dot(piece_rows, out_full, preferred_element_type=jnp.float32).astype(jnp.bfloat16),
        "wgt",
        scatter_dimension=0,
        tiled=True,
    ).astype(jnp.float32)
    tokens_out = share_rows // requests
    row_place = lax.axis_index("wgt") * share_rows
    base_rows = lax.dynamic_slice_in_dim(
        hidden.reshape(row_count, feat_width), row_place, share_rows, 0
    )
    residual = base_rows.reshape(tokens_out, requests, feat_width) + modulate[:, 2] * mixed.reshape(
        tokens_out, requests, feat_width
    )
    branch_in = (layer_norm(residual) * (1.0 + modulate[:, 6]) + modulate[:, 5]).astype(
        jnp.bfloat16
    )
    branch_rows = lax.all_gather(
        branch_in.reshape(share_rows, feat_width), "wgt", axis=0, tiled=True
    )
    expanded = jnp.dot(
        branch_rows,
        lax.all_gather(expand_weight, "seq", axis=0, tiled=True),
        preferred_element_type=jnp.float32,
    )
    expanded = jax.nn.gelu(expanded, approximate=True).astype(jnp.bfloat16)
    piece_rows = expanded
    branch = lax.psum_scatter(
        jnp.dot(piece_rows, contract_full, preferred_element_type=jnp.float32).astype(jnp.bfloat16),
        "wgt",
        scatter_dimension=0,
        tiled=True,
    ).astype(jnp.float32)
    second = residual + modulate[:, 7] * branch.reshape(tokens_out, requests, feat_width)
    final_in = (layer_norm(second) * (1.0 + modulate[:, 9]) + modulate[:, 8]).astype(jnp.bfloat16)
    own_velocity = jnp.dot(
        final_in.reshape(share_rows, feat_width), final_weight, preferred_element_type=jnp.float32
    ).reshape(tokens_out, requests, -1)
    guide_side = lax.axis_index("cfg")
    guided_count = latent.shape[1]
    kept_rows = lax.dynamic_slice_in_dim(own_velocity, guide_side * guided_count, guided_count, 1)
    sent_rows = lax.dynamic_slice_in_dim(
        own_velocity, (1 - guide_side) * guided_count, guided_count, 1
    )
    partner_velocity = from_partner(sent_rows, "cfg", 0)
    is_first = guide_side == 0
    conditional = jnp.where(is_first, kept_rows, partner_velocity)
    unconditional = jnp.where(is_first, partner_velocity, kept_rows)
    velocity = unconditional + guidance_scale * (conditional - unconditional)
    step_size = sigma_of(timesteps + 1) - sigma_of(timesteps)
    step_here = lax.dynamic_slice_in_dim(step_size, guide_side * guided_count, guided_count, 0)
    next_latent = latent + step_here[None, :, None] * velocity
    return (velocity, next_latent)


def solution(mesh):
    return jax.shard_map(
        body,
        mesh=mesh,
        in_specs=(
            P(("seq", "wgt"), "cfg", None),
            P("cfg", "seq", None, None),
            P("cfg", "seq", None),
            P("cfg", "seq"),
            P(),
            P("cfg", None, None, None),
            P(),
            P(None, "seq", "wgt"),
            P(None, "seq", "wgt"),
            P("wgt", "seq"),
            P("seq", "wgt"),
            P("wgt", "seq"),
            P(),
        ),
        out_specs=(P(("seq", "wgt"), "cfg", None), P(("seq", "wgt"), "cfg", None)),
        check_vma=False,
    )
```

profile of v0, /device:TPU:0, one launch (start us, length us, event | category | flops | bytes accessed | tf_op | source)
XLA Modules:
  0.0 821.4 jit_solution(10045632812660377062)
XLA Ops:
  16.4 163.7 %all-gather.8.cloned.1.call-done = bf16[5,2432,768]{2,1,0:T(8,128)(2,1)} async-done(((bf16[5,304,768]{2,1,0:T(8,128)(2,1)}), bf16[5,2432,768]{2,1,0:T(8,128)(2,1)}) %all-gather.8.cloned.1.call-update) | async-done | bytes 18677776 | tf_op jit(solution)/shard_map/all_gather | solution.py:80
  180.1 5.0 fusion.11
  198.6 6.7 add.222
  208.1 6.7 mul.301
  214.9 14.9 %fusion.6 = f32[512,3,768]{2,0,1:T(8,128)S(1)} fusion(bf16[5,2432,768]{2,1,0:T(8,128)(2,1)} %all-gather.8.cloned.1.call-done, f32[512,2432]{1,0:T(8,128)} %add.222, f32[512,2432]{1,0:T(8,128)} %mul.301, f32[512,2432]{1,0:T(8,128)} %reshape.249, f32[512]{0:T(512)S(1)} %rsqrt.60, f32[512]{0:T(512)S(1)} %div.60), kind=kOutput, calls=%fused_computation.9 | convolution fusion | flops 5744033792 | bytes 30871552 | tf_op jit(solution)/shard_map/rd,kdc->rkc/dot_general | solution.py:81
  245.8 14.4 %all-reduce = bf16[512]{0:T(512)(128)(2,1)S(1)} all-reduce(bf16[512]{0:T(512)(128)(2,1)S(1)} %dynamic-update-slice), channel_id=1, replica_groups=mesh['cfg'=2,'seq'=8,'wgt'=2] {'seq'}, use_global_device_ids=true, to_apply=%add | all-reduce | flops 512 | bytes 2048
  274.6 6.2 fusion.10
  280.8 78.5 %all-gather.10.cloned.1.call-done = bf16[1024,4,2,768]{0,3,1,2:T(8,128)(2,1)} async-done(((bf16[128,4,2,768]{0,3,1,2:T(8,128)(2,1)}), bf16[1024,4,2,768]{0,3,1,2:T(8,128)(2,1)}) %all-gather.10.cloned.1.call-update) | async-done | bytes 12582928 | tf_op jit(solution)/shard_map/all_gather | solution.py:106
  359.2 10.5 %fusion.76 = (bf16[1024,4,1,768]{0,3,1,2:T(8,128)(2,1)}, bf16[1024,4,1,768]{0,3,1,2:T(8,128)(2,1)}) fusion(bf16[1024,4,2,768]{0,3,1,2:T(8,128)(2,1)} %all-gather.10.cloned.1.call-done), kind=kLoop, calls=%fused_computation.131 | loop fusion | bytes 25165824 | tf_op jit(solution)/shard_map/slice | solution.py:110
  369.7 15.1 %multiply_reduce_fusion = (f32[4,12,128]{2,1,0:T(8,128)S(1)}, f32[4,12,128,1024]{3,2,1,0:T(8,128)}) fusion(bf16[1024,4,12,64]{0,3,2,1:T(8,128)(2,1)} %bitcast.131, f32[128,4,12,64]{0,3,2,1:T(8,128)S(1)} %copy.94, f32[64]{0:T(128)S(1)} %get-tuple-element.37, f32[128,4,12]{0,2,1:T(8,128)S(1)} %copy.93), kind=kOutput, calls=%fused_computation.1 | convolution fusion | flops 819062784 | bytes 33079552 | tf_op jit(solution)/shard_map/qrhd,krhd->rhqk/dot_general | solution.py:114
  384.9 4.0 fusion.8
  389.0 11.6 %fusion = f32[4,12,128]{2,1,0:T(8,128)S(1)} fusion(f32[4,12,128,1024]{3,2,1,0:T(8,128)} %get-tuple-element.40, f32[4,12,128]{2,1,0:T(8,128)S(1)} %fusion.64), kind=kLoop, calls=%fused_computation.2 | loop fusion | flops 18868224 | bytes 25214976 | tf_op jit(solution)/shard_map/reduce_sum | solution.py:127
  402.9 12.1 %fusion.35 = bf16[128,4,12,64]{0,3,2,1:T(8,128)(2,1)} fusion(f32[12,64,4,128]{3,1,0,2:T(8,128)} %fusion.13, bf16[1024,4,12,64]{0,3,2,1:T(8,128)(2,1)S(1)} %bitcast.134, f32[4,12,128,1024]{3,2,1,0:T(8,128)} %get-tuple-element.40, f32[4,12,128]{2,1,0:T(8,128)S(1)} %fusion.64, f32[128,4,12]{0,2,1:T(8,128)S(1)} %fusion.63), kind=kOutput, calls=%fused_computation.53 | convolution fusion | flops 825360384 | bytes 33865728 | tf_op jit(solution)/shard_map/rhqk,krhd->rhqd/dot_general | solution.py:128
  415.1 3.9 copy.106
  420.3 5.7 convolution_convert_fusion.1
  433.7 27.1 %reduce-scatter.3.cloned.1.call-done = bf16[256,2432]{1,0:T(8,128)(2,1)} async-done(((bf16[512,2432]{1,0:T(8,128)(2,1)}), bf16[256,2432]{1,0:T(8,128)(2,1)}) %reduce-scatter.3.cloned.1.call-update) | async-done | bytes 1245200 | tf_op jit(solution)/shard_map/reduce_scatter | solution.py:146
  468.4 119.9 %all-gather.18.cloned.1.call-done = bf16[2432,2816]{1,0:T(8,128)(2,1)} async-done(((bf16[304,2816]{1,0:T(8,128)(2,1)}), bf16[2432,2816]{1,0:T(8,128)(2,1)}) %all-gather.18.cloned.1.call-update) | async-done | bytes 13697040 | tf_op jit(solution)/shard_map/all_gather | solution.py:168
  588.3 37.4 %all-gather.16.cloned.1.call-done = bf16[512,2432]{1,0:T(8,128)(2,1)} async-done(((bf16[256,2432]{1,0:T(8,128)(2,1)}), bf16[512,2432]{1,0:T(8,128)(2,1)}) %all-gather.16.cloned.1.call-update) | async-done | bytes 2490384 | tf_op jit(solution)/shard_map/all_gather | solution.py:163
  625.7 13.9 %fusion.78 = f32[512,2816]{1,0:T(8,128)} fusion(bf16[512,2432]{1,0:T(8,128)(2,1)} %all-gather.16.cloned.1.call-done, bf16[2432,2816]{1,0:T(8,128)(2,1)} %all-gather.18.cloned.1.call-done), kind=kOutput, calls=%fused_computation.133 | convolution fusion | flops 7012876288 | bytes 21954560 | tf_op jit(solution)/shard_map/dot_general | solution.py:166
  639.6 113.8 %all-gather.20.cloned.1.call-done = bf16[2816,2432]{0,1:T(8,128)(2,1)} async-done(((bf16[2816,304]{0,1:T(8,128)(2,1)}), bf16[2816,2432]{0,1:T(8,128)(2,1)}) %all-gather.20.cloned.1.call-update) | async-done | bytes 13697040 | tf_op jit(solution)/shard_map/all_gather | solution.py:78
  753.4 15.0 %convolution_convert_fusion = bf16[512,2432]{1,0:T(8,128)(2,1)} fusion(bf16[2816,2432]{0,1:T(8,128)(2,1)} %all-gather.20.cloned.1.call-done, f32[512,2816]{1,0:T(8,128)} %fusion.78), kind=kOutput, calls=%fused_computation.31 | convolution fusion | flops 7027097600 | bytes 21954560 | tf_op jit(solution)/shard_map/dot_general | solution.py:174
  770.9 3.7 mul.338
  781.9 3.7 mul.357
  785.6 17.3 %reduce-scatter.5.cloned.1.call-done = bf16[256,2432]{1,0:T(8,128)(2,1)} async-done(((bf16[512,2432]{1,0:T(8,128)(2,1)}), bf16[256,2432]{1,0:T(8,128)(2,1)}) %reduce-scatter.5.cloned.1.call-update) | async-done | bytes 1245200 | tf_op jit(solution)/shard_map/reduce_scatter | solution.py:173
  (173 shorter events, 95.2 us)
Async XLA Ops:
  7.2 801.0 %copy-start = (bf16[2432,64]{0,1:T(8,128)(2,1)S(1)}, bf16[2432,64]{0,1:T(8,128)(2,1)}, u32[]{:S(2)}) copy-start(bf16[2432,64]{0,1:T(8,128)(2,1)} %param.25) | copy-start | bytes 933892
  7.2 3.5 copy-start.8
  7.2 172.9 %all-gather.8.cloned.1.call-start = ((), (), s32[]{:S(2)}) async-start(), calls=%async_computation.2 | async-start | bytes 21012480 | tf_op jit(solution)/shard_map/all_gather | solution.py:80
  10.6 259.0 %all-gather.12.cloned.1.call-start = ((), (), s32[]{:S(2)}) async-start(), calls=%async_computation.4 | async-start | bytes 1769472 | tf_op jit(solution)/shard_map/all_gather | solution.py:107
  189.8 169.5 %all-gather.10.cloned.1.call-start = ((), (), s32[]{:S(2)}) async-start(), calls=%async_computation.3 | async-start | bytes 14155776 | tf_op jit(solution)/shard_map/all_gather | solution.py:106
  198.6 6.7 copy-start.18
  242.3 18.0 %copy-start.6 = (f32[512,1,768]{2,0,1:T(8,128)S(1)}, f32[512,1,768]{2,0,1:T(8,128)}, u32[]{:S(2)}) copy-start(f32[512,1,768]{2,0,1:T(8,128)} %get-tuple-element.26) | copy-start | bytes 4718596
  243.6 176.7 %all-gather.14.cloned.1.call-start = ((), (), s32[]{:S(2)}) async-start(), calls=%async_computation.5 | async-start | bytes 4202496 | tf_op jit(solution)/shard_map/all_gather | solution.py:77
  244.2 216.6 %reduce-scatter.3.cloned.1.call-start = ((), (), s32[]{:S(2)}) async-start(), calls=%async_computation.6 | async-start | bytes 3735552 | tf_op jit(solution)/shard_map/reduce_scatter | solution.py:146
  369.7 15.1 %slice-start = ((s8[12582912]{0:T(1024)(128)(4,1)}), s8[4194304]{0:T(1024)(128)(4,1)S(1)}, s32[]{:S(2)}) async-start(s8[12582912]{0:T(1024)(128)(4,1)} %bitcast.129), calls=%async_computation.11 | async-start | bytes 8388608
  369.7 15.1 %slice-start.1 = ((s8[12582912]{0:T(1024)(128)(4,1)}), s8[4194304]{0:T(1024)(128)(4,1)S(1)}, s32[]{:S(2)}) async-start(s8[12582912]{0:T(1024)(128)(4,1)} %bitcast.129), calls=%async_computation.12 | async-start | bytes 8388608
  369.7 15.2 %slice-start.2 = ((s8[12582912]{0:T(1024)(128)(4,1)}), s8[4194304]{0:T(1024)(128)(4,1)S(1)}, s32[]{:S(2)}) async-start(s8[12582912]{0:T(1024)(128)(4,1)} %bitcast.129), calls=%async_computation.13 | async-start | bytes 8388608
  384.9 18.1 %slice-start.3 = ((s8[6291456]{0:T(1024)(128)(4,1)}), s8[2097152]{0:T(1024)(128)(4,1)S(1)}, s32[]{:S(2)}) async-start(s8[6291456]{0:T(1024)(128)(4,1)} %bitcast.132), calls=%async_computation.14 | async-start | bytes 4194304
  388.9 11.7 %copy-start.7 = (bf16[512,1,768]{0,2,1:T(8,128)(2,1)S(1)}, bf16[512,1,768]{0,2,1:T(8,128)(2,1)}, u32[]{:S(2)}) copy-start(bf16[512,1,768]{0,2,1:T(8,128)(2,1)} %copy.102) | copy-start | bytes 2359300
  389.0 14.0 %slice-start.4 = ((s8[6291456]{0:T(1024)(128)(4,1)}), s8[4194304]{0:T(1024)(128)(4,1)S(1)}, s32[]{:S(2)}) async-start(s8[6291456]{0:T(1024)(128)(4,1)} %bitcast.132), calls=%async_computation.15 | async-start | bytes 8388608
  426.1 162.2 %all-gather.18.cloned.1.call-start = ((), (), s32[]{:S(2)}) async-start(), calls=%async_computation.8 | async-start | bytes 15409152 | tf_op jit(solution)/shard_map/all_gather | solution.py:168
  426.7 199.1 %all-gather.16.cloned.1.call-start = ((), (), s32[]{:S(2)}) async-start(), calls=%async_computation.7 | async-start | bytes 3735552 | tf_op jit(solution)/shard_map/all_gather | solution.py:163
  460.8 3.8 copy-start.5
  467.6 285.7 %all-gather.20.cloned.1.call-start = ((), (), s32[]{:S(2)}) async-start(), calls=%async_computation.9 | async-start | bytes 15409152 | tf_op jit(solution)/shard_map/all_gather | solution.py:78
  468.4 334.5 %reduce-scatter.5.cloned.1.call-start = ((), (), s32[]{:S(2)}) async-start(), calls=%async_computation.10 | async-start | bytes 3735552 | tf_op jit(solution)/shard_map/reduce_scatter | solution.py:173
  770.9 3.7 copy-start.13
  776.5 3.7 copy-start.12
  807.8 5.2 copy-start.20
  808.7 4.3 collective-permute-start
  (16 other events, 35.5 us)
Sparse Core Ops, SparseCore 0:
  10.7 169.3 all-gather.7
  189.9 23.2 all-gather.11
  243.7 115.4 all-gather.9
  360.7 41.3 all-gather.13
  426.2 34.5 reduce-scatter.2
  462.4 125.8 all-gather.17
  589.9 35.7 all-gather.15
  627.5 125.8 all-gather.19
  768.5 34.3 reduce-scatter.4
where the time goes:
time: 827 us; the launch traced here: 821 us
  waiting for transfers between devices  562 us (68%)
  matrix products  92.4 us (11%)
  local copies, waits for them, and re-layouts  88.6 us (11%)
  other arithmetic  46.4 us (6%)
  between operations  15.5 us (2%)
  blocking collectives  14.4 us (2%)
    all_gather x1, waiting for transfers between devices, body(): piece = lax.all_gather(all_weights, 'seq', axis=1, tiled=True)  164 us
    all_gather x1, waiting for transfers between devices, body(): lax.all_gather(expand_weight, 'seq', axis=0, tiled=True)  120 us
    all_gather x1, waiting for transfers between devices, body(): lax.all_gather(contract_weight, 'seq', axis=1, tiled=True)  114 us
    all_gather x1, waiting for transfers between devices, body(): image_piece = lax.all_gather(image_pair, 'seq', axis=0, tiled=True)  78.5 us
    all_gather x1, waiting for transfers between devices, body(): lax.all_gather(branch_in.reshape(share_rows, feat_width), 'wgt', axis=0,...  37.4 us
    reduce_scatter x1, waiting for transfers between devices, body(): lax.psum_scatter(jnp.dot(piece_rows, out_full, preferred_element_type=jnp...  27.1 us
    reduce_scatter x1, waiting for transfers between devices, body(): lax.psum_scatter(jnp.dot(piece_rows, contract_full, preferred_element_typ...  17.3 us
  transfers between devices with their start and end apart: 10, of which 8 were waited for; matrix products, arithmetic and copies ran while one was open for 22% of the time, Pallas kernels for 0%

commit v1 on v0

--- a/solution.py
+++ b/solution.py
@@ -1,6 +1,8 @@
 import jax
 import jax.numpy as jnp
 from jax import lax
+from jax.experimental import pallas as pl
+from jax.experimental.pallas import tpu as pltpu
 from jax.sharding import PartitionSpec as P
 
 STEPS = 28
@@ -25,6 +27,12 @@
     return centred * lax.rsqrt(spread + eps_norm)
 
 
+def rows_by_rows(left, right):
+    return lax.dot_general(
+        left, right, (((1,), (1,)), ((), ())), preferred_element_type=jnp.float32
+    )
+
+
 def head_norm(values, gain_row):
     power = jnp.mean(values * values, axis=-1, keepdims=True)
     return values * lax.rsqrt(power + eps_norm) * gain_row
@@ -33,6 +41,193 @@
 def sigma_of(index_row):
     time_left = 1.0 - index_row.astype(jnp.float32) / STEPS
     return flow_shift * time_left / (1.0 + (flow_shift - 1.0) * time_left)
+
+
+def gather_kernel(count, seq_size, *refs):
+    ins, outs = refs[:count], refs[count : 2 * count]
+    z_send, z_recv, x_send, x_recv, c_send, c_recv, own_send, own_recv, local_sem = refs[2 * count :]
+    span = seq_size // 2
+    me, side = lax.axis_index("seq"), lax.axis_index("cfg")
+    place, core = me // 2, me % 2
+    partner_core = me + 1 - 2 * core
+
+    def half_lanes(ref, half):
+        width = ref.shape[-1] // 2
+        return pl.ds(pl.multiple_of(half * width, 128), width)
+
+    def shard(item, index, half=None):
+        rows = ins[item].shape[1]
+        at_rows = pl.ds(pl.multiple_of(index * rows, 16), rows)
+        if half is None:
+            return outs[item].at[:, at_rows, :]
+        return outs[item].at[:, at_rows, half_lanes(outs[item], half)]
+
+    def origin(way, dist):
+        return me - 2 * dist if way == 0 else me + 2 * dist
+
+    def exists(way, dist):
+        return place - dist >= 0 if way == 0 else place + dist < span
+
+    def hop(item, way, dist):
+        if dist == 0:
+            source = ins[item].at[:, :, half_lanes(ins[item], side)]
+        else:
+            source = shard(item, origin(way, dist), side)
+        return pltpu.make_async_remote_copy(
+            src_ref=source,
+            dst_ref=shard(item, origin(way, dist), side),
+            send_sem=z_send.at[item, way, dist],
+            recv_sem=z_recv.at[item, way, dist],
+            device_id={"seq": me + 2 if way == 0 else me - 2},
+            device_id_type=pl.DeviceIdType.MESH,
+        )
+
+    def landed(item, way, dist):
+        here = shard(item, origin(way, dist), side)
+        return pltpu.make_async_remote_copy(
+            src_ref=here,
+            dst_ref=here,
+            send_sem=z_send.at[item, way, dist - 1],
+            recv_sem=z_recv.at[item, way, dist - 1],
+            device_id={"cfg": 1 - side},
+            device_id_type=pl.DeviceIdType.MESH,
+        )
+
+    def across(item, way, dist, half):
+        here = shard(item, origin(way, dist), half)
+        return pltpu.make_async_remote_copy(
+            src_ref=here,
+            dst_ref=here,
+            send_sem=x_send.at[item, way, dist],
+            recv_sem=x_recv.at[item, way, dist],
+            device_id={"cfg": 1 - side},
+            device_id_type=pl.DeviceIdType.MESH,
+        )
+
+    def to_core(item, way, dist, home):
+        here = shard(item, origin(way, dist) - me + home)
+        return pltpu.make_async_remote_copy(
+            src_ref=here,
+            dst_ref=here,
+            send_sem=c_send.at[item, way, dist],
+            recv_sem=c_recv.at[item, way, dist],
+            device_id={"seq": partner_core},
+            device_id_type=pl.DeviceIdType.MESH,
+        )
+
+    def own_to_core(item, home):
+        return pltpu.make_async_remote_copy(
+            src_ref=ins[item],
+            dst_ref=shard(item, home),
+            send_sem=own_send.at[item],
+            recv_sem=own_recv.at[item],
+            device_id={"seq": partner_core},
+            device_id_type=pl.DeviceIdType.MESH,
+        )
+
+    def local(item):
+        return pltpu.make_async_copy(ins[item], shard(item, me), local_sem.at[item])
+
+    barrier = pltpu.get_barrier_semaphore()
+    pl.semaphore_signal(barrier, device_id={"cfg": 1 - side}, device_id_type=pl.DeviceIdType.MESH)
+    pl.semaphore_signal(barrier, device_id={"seq": partner_core}, device_id_type=pl.DeviceIdType.MESH)
+    for way in (0, 1):
+
+        @pl.when(exists(1 - way, 1))
+        def _():
+            pl.semaphore_signal(
+                barrier,
+                device_id={"seq": me + 2 if way == 0 else me - 2},
+                device_id_type=pl.DeviceIdType.MESH,
+            )
+
+    peers = 2 + lax.min(place, 1) + lax.min(span - 1 - place, 1)
+    pl.semaphore_wait(barrier, peers)
+
+    for item in range(count):
+        for way in (0, 1):
+
+            @pl.when(exists(1 - way, 1))
+            def _():
+                hop(item, way, 0).start()
+
+    for item in range(count):
+        own_to_core(item, me).start()
+        local(item).start()
+
+    def pass_to_core(item, dist):
+        for way in (0, 1):
+
+            @pl.when(exists(way, dist))
+            def _():
+                across(item, way, dist, 1 - side).wait_recv()
+                to_core(item, way, dist, me).start()
+
+    for dist in range(1, span):
+        for item in range(count):
+            for way in (0, 1):
+
+                @pl.when(exists(way, dist))
+                def _():
+                    landed(item, way, dist).wait_recv()
+
+                    @pl.when(exists(1 - way, 1))
+                    def _():
+                        hop(item, way, dist).start()
+
+                    across(item, way, dist, side).start()
+
+            if dist > 1:
+                pass_to_core(item, dist - 1)
+    for item in range(count):
+        pass_to_core(item, span - 1)
+
+    for item in range(count):
+        own_to_core(item, partner_core).wait_recv()
+        own_to_core(item, me).wait_send()
+        local(item).wait()
+        for way in (0, 1):
+
+            @pl.when(exists(1 - way, 1))
+            def _():
+                hop(item, way, 0).wait_send()
+
+            for dist in range(1, span):
+
+                @pl.when(exists(way, dist))
+                def _():
+                    @pl.when(exists(1 - way, 1))
+                    def _():
+                        hop(item, way, dist).wait_send()
+
+                    across(item, way, dist, side).wait_send()
+                    to_core(item, way, dist, me).wait_send()
+                    to_core(item, way, dist, partner_core).wait_recv()
+
+
+def gather_rows(arrays, collective_id):
+    seq_size = lax.axis_size("seq")
+    fits = lax.axis_size("cfg") == 2 and seq_size <= 8 and seq_size % 2 == 0
+    for array in arrays:
+        fits = fits and array.shape[1] % 16 == 0 and array.shape[2] % 256 == 0
+    if not fits:
+        return [lax.all_gather(array, "seq", axis=1, tiled=True) for array in arrays]
+    count, span = len(arrays), seq_size // 2
+    dma = pltpu.SemaphoreType.DMA
+    whole = [(a.shape[0], a.shape[1] * seq_size, a.shape[2]) for a in arrays]
+    moved = sum(2 * a.size * seq_size for a in arrays)
+    return pl.pallas_call(
+        lambda *refs: gather_kernel(count, seq_size, *refs),
+        out_shape=[jax.ShapeDtypeStruct(s, jnp.bfloat16) for s in whole],
+        in_specs=[pl.BlockSpec(memory_space=pl.ANY)] * count,
+        out_specs=[pl.BlockSpec(memory_space=pl.ANY)] * count,
+        scratch_shapes=[dma((count, 2, span))] * 6 + [dma((count,))] * 3,
+        compiler_params=pltpu.CompilerParams(
+            collective_id=collective_id, has_side_effects=True
+        ),
+        cost_estimate=pl.CostEstimate(flops=0, bytes_accessed=2 * moved, transcendentals=0),
+        name="gather_rows",
+    )(*arrays)
 
 
 def body(
@@ -72,17 +267,21 @@
     text_normed = (
         layer_norm(txt_hidden[0].astype(jnp.float32)) * (1.0 + text_mod[:, 1]) + text_mod[:, 0]
     ).astype(jnp.bfloat16)
-    all_weights = jnp.concatenate([qkv_weight, text_weight], axis=0)
-    out_full, contract_full = (
-        lax.all_gather(out_weight, "seq", axis=1, tiled=True),
-        lax.all_gather(contract_weight, "seq", axis=1, tiled=True),
-    )
-    piece = lax.all_gather(all_weights, "seq", axis=1, tiled=True)
+    qkv_full, text_full, out_full, contract_full, expand_full = gather_rows(
+        [
+            qkv_weight,
+            text_weight,
+            out_weight.T[None],
+            contract_weight.T[None],
+            expand_weight[None],
+        ],
+        0,
+    )
     image_term = jnp.einsum(
-        "rd,kdc->rkc", token_rows, piece[:3], preferred_element_type=jnp.float32
+        "rd,kdc->rkc", token_rows, qkv_full, preferred_element_type=jnp.float32
     )
     text_term = jnp.einsum(
-        "rd,kdc->rkc", text_normed, piece[3:], preferred_element_type=jnp.float32
+        "rd,kdc->rkc", text_normed, text_full, preferred_element_type=jnp.float32
     )
     queries = head_norm(
         image_term[:, 0].reshape(tokens_here, requests, heads_here, head_size), qk_gain[0]
@@ -103,9 +302,20 @@
     scale_factor = head_size ** (-0.5)
     request_ids = jnp.arange(requests, dtype=jnp.float32)
     running_max = jnp.full((requests, heads_here, tokens_here), masked_score, jnp.float32)
-    image_piece = lax.all_gather(image_pair, "seq", axis=0, tiled=True)
-    text_piece = lax.all_gather(text_pair, "seq", axis=0, tiled=True)
-    owner_piece = lax.all_gather(text_owner, "seq", axis=0, tiled=True)
+    pair_cols = 2 * local_cols
+    owner_row = jnp.pad(text_owner, (0, pair_cols - text_here))[None]
+    packed = jnp.concatenate(
+        [
+            image_pair.reshape(row_count, pair_cols),
+            text_pair.reshape(text_here, pair_cols),
+            owner_row,
+        ],
+        axis=0,
+    )
+    gathered = lax.all_gather(packed, "seq", axis=0)
+    image_piece = gathered[:, :row_count].reshape(-1, requests, 2, local_cols)
+    text_piece = gathered[:, row_count : row_count + text_here].reshape(-1, 2, local_cols)
+    owner_piece = gathered[:, row_count + text_here, :text_here].reshape(-1)
     piece_keys = image_piece[:, :, 0].reshape(-1, requests, heads_here, head_size)
     piece_values = image_piece[:, :, 1].reshape(-1, requests, heads_here, head_size)
     text_keys = text_piece[:, 0].reshape(-1, heads_here, head_size)
@@ -144,7 +354,7 @@
     share_rows = row_count // lax.axis_size("wgt")
     piece_rows = attended
     mixed = lax.psum_scatter(
-        jnp.dot(piece_rows, out_full, preferred_element_type=jnp.float32).astype(jnp.bfloat16),
+        rows_by_rows(piece_rows, out_full[0]).astype(jnp.bfloat16),
         "wgt",
         scatter_dimension=0,
         tiled=True,
@@ -165,13 +375,13 @@
     )
     expanded = jnp.dot(
         branch_rows,
-        lax.all_gather(expand_weight, "seq", axis=0, tiled=True),
+        expand_full[0],
         preferred_element_type=jnp.float32,
     )
     expanded = jax.nn.gelu(expanded, approximate=True).astype(jnp.bfloat16)
     piece_rows = expanded
     branch = lax.psum_scatter(
-        jnp.dot(piece_rows, contract_full, preferred_element_type=jnp.float32).astype(jnp.bfloat16),
+        rows_by_rows(piece_rows, contract_full[0]).astype(jnp.bfloat16),
         "wgt",
         scatter_dimension=0,
         tiled=True,

time: 827 us -> 809 us (0.978)
  waiting for transfers between devices: 562 us -> 206 us
  Pallas kernels: 0 us -> 231 us
  local copies, waits for them, and re-layouts: 88.6 us -> 216 us
  blocking collectives: 14.4 us -> 0 us
    all_gather x6 -> x1, waiting for transfers between devices: 476 us -> 120 us  [body(): gathered = lax.all_gather(packed, 'seq', axis=0)]
    pallas_call x0 -> x1, Pallas kernels: none -> 231 us  [gather_rows(): pl.pallas_call(lambda *refs: gather_kernel(count, seq_size, *refs), out_s...]
    slice x1 -> x2, local copies, waits for them, and re-layouts: 10.5 us -> 54.1 us  [body(): image_piece[:, :, 1].reshape(-1, requests, heads_here, head_size)]
    slice x0 -> x3, local copies, waits for them, and re-layouts: none -> 42.7 us  [the longest x1 29.4 us: body(): image_piece[:, :, 0].reshape(-1, requests, heads_here, head_size)]
    reshape x0 -> x3, local copies, waits for them, and re-layouts: none -> 29.4 us  [the longest x1 25.7 us: body(): image_piece = gathered[:, :row_count].reshape(-1, requests, 2, local_cols)]
    unnamed x1 -> x0, blocking collectives: 14.4 us -> none
  transfers between devices with their start and end apart: 10 -> 5, of which waited for: 8 -> 5; matrix products, arithmetic and copies ran while one was open for 22% -> 4% of each run, Pallas kernels for 0% -> 0%
where the time goes in v1:
time: 809 us; the launch traced here: 800 us
  Pallas kernels  231 us (29%)
  local copies, waits for them, and re-layouts  216 us (27%)
  waiting for transfers between devices  206 us (25%)
  matrix products  84.3 us (10%)
  other arithmetic  45.2 us (6%)
  between operations  14.6 us (2%)
    pallas_call x1, Pallas kernels, gather_rows(): pl.pallas_call(lambda *refs: gather_kernel(count, seq_size, *refs), out_s...  231 us
    all_gather x1, waiting for transfers between devices, body(): gathered = lax.all_gather(packed, 'seq', axis=0)  120 us
    slice x2, local copies, waits for them, and re-layouts, body(): image_piece[:, :, 1].reshape(-1, requests, heads_here, head_size)  54.1 us
    all_gather x1, waiting for transfers between devices, body(): lax.all_gather(branch_in.reshape(share_rows, feat_width), 'wgt', axis=0,...  37.7 us
    slice x1, local copies, waits for them, and re-layouts, body(): image_piece[:, :, 0].reshape(-1, requests, heads_here, head_size)  29.4 us
    reduce_scatter x1, waiting for transfers between devices, body(): lax.psum_scatter(rows_by_rows(piece_rows, out_full[0]).astype(jnp.bfloat1...  26.7 us
    reshape x1, local copies, waits for them, and re-layouts, body(): image_piece = gathered[:, :row_count].reshape(-1, requests, 2, local_cols)  25.7 us
    reduce_scatter x1, waiting for transfers between devices, body(): lax.psum_scatter(rows_by_rows(piece_rows, contract_full[0]).astype(jnp.bf...  19.1 us
  transfers between devices with their start and end apart: 5, of which 5 were waited for; matrix products, arithmetic and copies ran while one was open for 4% of the time, Pallas kernels for 0%

profile of v1, /device:TPU:0, one launch (start us, length us, event | category | flops | bytes accessed | tf_op | source)
XLA Modules:
  0.0 799.7 jit_solution(3989188992389806334)
XLA Ops:
  7.2 5.5 reshape.272
  19.2 6.7 add.224
  28.7 6.7 mul.301
  35.5 231.4 %gather_rows.1 = (bf16[3,2432,768]{2,1,0:T(8,128)(2,1)}, bf16[2,2432,768]{2,1,0:T(8,128)(2,1)}, bf16[1,2432,768]{2,1,0:T(8,128)(2,1)}, bf16[1,2432,2816]{2,1,0:T(8,128)(2,1)}, bf16[1,2432,2816]{2,1,0:T(8,128)(2,1)}) custom-call(bf16[3,304,768]{2,1,0:T(8,128)(2,1)} %refs_0_.1, bf16[2,304,768]{2,1,0:T(8,128)(2,1)} %refs_1_.1, bf16[1,304,768]{2,1,0:T(8,128)(2,1)} %bitcast.165, ...), custom_call_target="tpu_custom_call" | custom-call | bytes 99614720 | tf_op jit(solution)/shard_map/gather_rows/pallas_call | solution.py:219
  266.9 14.8 %fusion.32 = f32[512,3,768]{2,0,1:T(8,128)S(1)} fusion(bf16[3,2432,768]{2,1,0:T(8,128)(2,1)} %get-tuple-element.7, f32[512,2432]{1,0:T(8,128)} %add.224, f32[512,2432]{1,0:T(8,128)} %mul.301, f32[512,2432]{1,0:T(8,128)} %reshape.272, f32[512]{0:T(512)S(1)} %rsqrt.60, f32[512]{0:T(512)S(1)} %div.60), kind=kOutput, calls=%fused_computation.36 | convolution fusion | flops 5744033792 | bytes 30871552 | tf_op jit(solution)/shard_map/rd,kdc->rkc/dot_general | solution.py:280
  314.3 4.0 multiply_reduce_fusion.1
  318.4 120.0 %all-gather.7.cloned.1.call-done = bf16[8,577,1536]{2,1,0:T(8,128)(2,1)} async-done(((bf16[1,577,1536]{2,1,0:T(8,128)(2,1)}), bf16[8,577,1536]{2,1,0:T(8,128)(2,1)}) %all-gather.7.cloned.1.call-update) | async-done | bytes 14180368 | tf_op jit(solution)/shard_map/all_gather | solution.py:315
  452.6 10.6 %slice.114 = bf16[8,512,1536]{2,1,0:T(8,128)(2,1)} slice(bf16[8,577,1536]{2,1,0:T(8,128)(2,1)} %all-gather.7.cloned.1.call-done), slice={[0:8], [0:512], [0:1536]} | slice | bytes 25165824 | tf_op jit(solution)/shard_map/slice | solution.py:316
  463.2 25.7 %reshape.270 = bf16[1024,4,2,768]{3,2,1,0:T(2,128)(2,1)} reshape(bf16[8,512,1536]{2,1,0:T(8,128)(2,1)} %slice.114) | data formatting | bytes 25165824 | tf_op jit(solution)/shard_map/reshape | solution.py:316
  488.9 24.7 %fusion.76 = (bf16[1024,4,1,768]{3,2,1,0:T(2,128)(2,1)}, bf16[1024,4,1,768]{3,2,1,0:T(2,128)(2,1)}) fusion(bf16[1024,4,2,768]{3,2,1,0:T(2,128)(2,1)} %reshape.270), kind=kLoop, calls=%fused_computation.128 | loop fusion | bytes 25165824 | tf_op jit(solution)/shard_map/slice | solution.py:320
  513.6 29.4 %copy.113 = bf16[1024,4,1,768]{0,3,1,2:T(8,128)(2,1)} copy(bf16[1024,4,1,768]{3,2,1,0:T(2,128)(2,1)} %get-tuple-element.33) | data formatting | bytes 12582912 | tf_op jit(solution)/shard_map/slice | solution.py:319
  543.0 14.6 %multiply_reduce_fusion = (f32[4,12,128]{2,1,0:T(8,128)S(1)}, f32[4,12,128,1024]{3,2,1,0:T(8,128)}) fusion(bf16[1024,4,12,64]{0,3,2,1:T(8,128)(2,1)} %bitcast.156, f32[128,4,12,64]{0,3,2,1:T(8,128)S(1)} %copy.106, f32[64]{0:T(128)S(1)} %copy-done.23, f32[128,4,12]{0,2,1:T(8,128)S(1)} %copy.105), kind=kOutput, calls=%fused_computation.1 | convolution fusion | flops 819062784 | bytes 33079552 | tf_op jit(solution)/shard_map/qrhd,krhd->rhqk/dot_general | solution.py:324
  557.7 6.5 fusion.12
  564.2 11.1 %fusion = f32[4,12,128]{2,1,0:T(8,128)S(1)} fusion(f32[4,12,128,1024]{3,2,1,0:T(8,128)} %get-tuple-element.50, f32[4,12,128]{2,1,0:T(8,128)S(1)} %fusion.67), kind=kLoop, calls=%fused_computation.2 | loop fusion | flops 18868224 | bytes 25214976 | tf_op jit(solution)/shard_map/reduce_sum | solution.py:337
  578.5 29.4 %copy.117 = bf16[1024,4,1,768]{0,3,1,2:T(8,128)(2,1)} copy(bf16[1024,4,1,768]{3,2,1,0:T(2,128)(2,1)} %get-tuple-element.32) | data formatting | bytes 12582912 | tf_op jit(solution)/shard_map/slice | solution.py:320
  607.9 7.2 fusion.10
  618.5 12.1 %fusion.37 = bf16[128,4,12,64]{0,3,2,1:T(8,128)(2,1)} fusion(f32[12,64,4,128]{3,1,0,2:T(8,128)} %fusion.13, bf16[1024,4,12,64]{0,3,2,1:T(8,128)(2,1)S(1)} %bitcast.159, f32[4,12,128,1024]{3,2,1,0:T(8,128)} %get-tuple-element.50, f32[4,12,128]{2,1,0:T(8,128)S(1)} %fusion.67, f32[128,4,12]{0,2,1:T(8,128)S(1)} %fusion.66), kind=kOutput, calls=%fused_computation.51 | convolution fusion | flops 825360384 | bytes 33865728 | tf_op jit(solution)/shard_map/rhqk,krhd->rhqd/dot_general | solution.py:338
  630.6 3.9 copy.122
  635.8 5.7 convolution_convert_fusion
  649.4 26.7 %reduce-scatter.3.cloned.1.call-done = bf16[256,2432]{1,0:T(8,128)(2,1)} async-done(((bf16[512,2432]{1,0:T(8,128)(2,1)}), bf16[256,2432]{1,0:T(8,128)(2,1)}) %reduce-scatter.3.cloned.1.call-update) | async-done | bytes 1245200 | tf_op jit(solution)/shard_map/reduce_scatter | solution.py:356
  683.0 37.7 %all-gather.5.cloned.1.call-done = bf16[512,2432]{1,0:T(8,128)(2,1)} async-done(((bf16[256,2432]{1,0:T(8,128)(2,1)}), bf16[512,2432]{1,0:T(8,128)(2,1)}) %all-gather.5.cloned.1.call-update) | async-done | bytes 2490384 | tf_op jit(solution)/shard_map/all_gather | solution.py:373
  720.6 12.5 %fusion.22 = bf16[512,2816]{1,0:T(8,128)(2,1)S(1)} fusion(bf16[512,2432]{1,0:T(8,128)(2,1)} %all-gather.5.cloned.1.call-done, bf16[1,2432,2816]{2,1,0:T(8,128)(2,1)} %get-tuple-element.10), kind=kOutput, calls=%fused_computation.26 | convolution fusion | flops 7025852416 | bytes 19070976 | tf_op jit(solution)/shard_map/dot_general | solution.py:376
  733.1 12.0 %fusion.25 = bf16[512,2432]{1,0:T(8,128)(2,1)} fusion(bf16[512,2816]{1,0:T(8,128)(2,1)S(1)} %fusion.22, bf16[1,2432,2816]{2,1,0:T(8,128)(2,1)} %get-tuple-element.11), kind=kOutput, calls=%fused_computation.31 | convolution fusion | flops 7014121472 | bytes 19070976 | tf_op jit(solution)/shard_map/dot_general | solution.py:31
  762.4 19.1 %reduce-scatter.5.cloned.1.call-done = bf16[256,2432]{1,0:T(8,128)(2,1)} async-done(((bf16[512,2432]{1,0:T(8,128)(2,1)}), bf16[256,2432]{1,0:T(8,128)(2,1)}) %reduce-scatter.5.cloned.1.call-update) | async-done | bytes 1245200 | tf_op jit(solution)/shard_map/reduce_scatter | solution.py:383
  (159 shorter events, 107.1 us)
Async XLA Ops:
  7.2 779.6 %copy-start = (bf16[2432,64]{0,1:T(8,128)(2,1)S(1)}, bf16[2432,64]{0,1:T(8,128)(2,1)}, u32[]{:S(2)}) copy-start(bf16[2432,64]{0,1:T(8,128)(2,1)} %param.25) | copy-start | bytes 933892
  7.2 5.5 copy-start.1
  7.2 431.3 %all-gather.7.cloned.1.call-start = ((), (), s32[]{:S(2)}) async-start(), calls=%async_computation.5 | async-start | bytes 16146432 | tf_op jit(solution)/shard_map/all_gather | solution.py:315
  12.7 2.9 copy-start.14
  281.8 2.5 copy-start.24
  281.8 4.7 copy-start.6
  283.3 2.7 copy-start.13
  306.5 2.1 copy-start.9
  307.9 368.2 %reduce-scatter.3.cloned.1.call-start = ((), (), s32[]{:S(2)}) async-start(), calls=%async_computation.2 | async-start | bytes 3735552 | tf_op jit(solution)/shard_map/reduce_scatter | solution.py:356
  513.6 29.4 %copy-start.23 = (f32[64]{0:T(128)S(1)}, f32[64]{0:T(128)}, u32[]{:S(2)}) copy-start(f32[64]{0:T(128)} %get-tuple-element.47) | copy-start | bytes 772
  564.2 11.1 %copy-start.7 = (bf16[512,1,768]{2,1,0:T(2,128)(2,1)S(1)}, bf16[512,1,768]{2,1,0:T(2,128)(2,1)}, u32[]{:S(2)}) copy-start(bf16[512,1,768]{2,1,0:T(2,128)(2,1)} %get-tuple-element.38) | copy-start | bytes 2359300
  607.9 7.2 copy-start.12
  615.1 3.4 copy-start.8
  641.6 79.0 %all-gather.5.cloned.1.call-start = ((), (), s32[]{:S(2)}) async-start(), calls=%async_computation.3 | async-start | bytes 3735552 | tf_op jit(solution)/shard_map/all_gather | solution.py:373
  642.7 2.1 copy-start.19
  645.1 2.0 copy-start.18
  676.1 3.8 copy-start.5
  682.9 98.5 %reduce-scatter.5.cloned.1.call-start = ((), (), s32[]{:S(2)}) async-start(), calls=%async_computation.4 | async-start | bytes 3735552 | tf_op jit(solution)/shard_map/reduce_scatter | solution.py:383
  747.7 3.7 copy-start.16
  753.2 3.7 copy-start.15
  781.5 3.0 copy-start.3
  786.4 2.4 copy-start.26
  786.4 5.2 copy-start.21
  787.2 4.3 collective-permute-start
  (8 other events, 11.1 us)
Sparse Core Ops, SparseCore 0:
  308.0 130.4 all-gather.6
  641.7 34.3 reduce-scatter.2
  683.0 37.5 all-gather.4
  745.3 36.1 reduce-scatter.4

commit v2 on v1

--- a/solution.py
+++ b/solution.py
@@ -267,16 +267,10 @@
     text_normed = (
         layer_norm(txt_hidden[0].astype(jnp.float32)) * (1.0 + text_mod[:, 1]) + text_mod[:, 0]
     ).astype(jnp.bfloat16)
-    qkv_full, text_full, out_full, contract_full, expand_full = gather_rows(
-        [
-            qkv_weight,
-            text_weight,
-            out_weight.T[None],
-            contract_weight.T[None],
-            expand_weight[None],
-        ],
-        0,
-    )
+    owner_piece = lax.all_gather(
+        segments[0].astype(jnp.float32).astype(jnp.bfloat16), "seq", axis=0, tiled=True
+    )
+    qkv_full, text_full = gather_rows([qkv_weight, text_weight], 0)
     image_term = jnp.einsum(
         "rd,kdc->rkc", token_rows, qkv_full, preferred_element_type=jnp.float32
     )
@@ -298,24 +292,20 @@
         [keys_img.reshape(tokens_here, requests, local_cols), values_img], axis=2
     )
     text_pair = jnp.stack([keys_txt.reshape(text_here, local_cols), values_txt], axis=1)
-    text_owner = segment_row.astype(jnp.float32).astype(jnp.bfloat16)
     scale_factor = head_size ** (-0.5)
     request_ids = jnp.arange(requests, dtype=jnp.float32)
     running_max = jnp.full((requests, heads_here, tokens_here), masked_score, jnp.float32)
-    pair_cols = 2 * local_cols
-    owner_row = jnp.pad(text_owner, (0, pair_cols - text_here))[None]
-    packed = jnp.concatenate(
-        [
-            image_pair.reshape(row_count, pair_cols),
-            text_pair.reshape(text_here, pair_cols),
-            owner_row,
-        ],
-        axis=0,
-    )
-    gathered = lax.all_gather(packed, "seq", axis=0)
-    image_piece = gathered[:, :row_count].reshape(-1, requests, 2, local_cols)
-    text_piece = gathered[:, row_count : row_count + text_here].reshape(-1, 2, local_cols)
-    owner_piece = gathered[:, row_count + text_here, :text_here].reshape(-1)
+    image_piece = lax.all_gather(image_pair, "seq", axis=0, tiled=True)
+    text_piece = lax.all_gather(text_pair, "seq", axis=0, tiled=True)
+    late_weights, _ = lax.optimization_barrier(
+        ((out_weight, contract_weight, expand_weight), image_pair)
+    )
+    late_full = gather_rows(
+        [late_weights[0].T[None], late_weights[1].T[None], late_weights[2][None]], 1
+    )
+    (out_full, contract_full, expand_full), queries = lax.optimization_barrier(
+        (tuple(late_full), queries)
+    )
     piece_keys = image_piece[:, :, 0].reshape(-1, requests, heads_here, head_size)
     piece_values = image_piece[:, :, 1].reshape(-1, requests, heads_here, head_size)
     text_keys = text_piece[:, 0].reshape(-1, heads_here, head_size)

time: 809 us -> 703 us (0.87)
  local copies, waits for them, and re-layouts: 216 us -> 86.3 us
  Pallas kernels: 231 us -> 355 us
  waiting for transfers between devices: 206 us -> 87.8 us
  blocking collectives: 0 us -> 16.1 us
    pallas_call x1 -> x2, Pallas kernels: 231 us -> 355 us  [gather_rows(): pl.pallas_call(lambda *refs: gather_kernel(count, seq_size, *refs), out_s...]
    all_gather x1 -> x2, waiting for transfers between devices: 120 us -> 0.01 us  [the longest x1 0.01 us: body(): text_piece = lax.all_gather(text_pair, 'seq', axis=0, tiled=True)]
    slice x2 -> x1, local copies, waits for them, and re-layouts: 54.1 us -> 10.4 us  [body(): image_piece[:, :, 1].reshape(-1, requests, heads_here, head_size)]
    slice x3 -> x0, local copies, waits for them, and re-layouts: 42.7 us -> none  [the longest x1 29.4 us: body(): image_piece[:, :, 0].reshape(-1, requests, heads_here, head_size)]
    reshape x3 -> x0, local copies, waits for them, and re-layouts: 29.4 us -> none  [the longest x1 25.7 us: body(): image_piece = gathered[:, :row_count].reshape(-1, requests, 2, local_cols)]
    unnamed x0 -> x1, blocking collectives: none -> 16.1 us
  transfers between devices with their start and end apart: 5 -> 6, of which waited for: 5 -> 4; matrix products, arithmetic and copies ran while one was open for 4% -> 15% of each run, Pallas kernels for 0% -> 36%
where the time goes in v2:
time: 703 us; the launch traced here: 697 us
  Pallas kernels  355 us (50%)
  matrix products  87.9 us (13%)
  waiting for transfers between devices  87.8 us (12%)
  local copies, waits for them, and re-layouts  86.3 us (12%)
  other arithmetic  46.8 us (7%)
  blocking collectives  16.1 us (2%)
  between operations  15.5 us (2%)
    pallas_call x2, Pallas kernels, gather_rows(): pl.pallas_call(lambda *refs: gather_kernel(count, seq_size, *refs), out_s...  355 us
    all_gather x1, waiting for transfers between devices, body(): lax.all_gather(branch_in.reshape(share_rows, feat_width), 'wgt', axis=0,...  37.7 us
    reduce_scatter x1, waiting for transfers between devices, body(): lax.psum_scatter(rows_by_rows(piece_rows, out_full[0]).astype(jnp.bfloat1...  27.5 us
    reduce_scatter x1, waiting for transfers between devices, body(): lax.psum_scatter(rows_by_rows(piece_rows, contract_full[0]).astype(jnp.bf...  19.9 us
    dot_general x2, matrix products, rows_by_rows(): lax.dot_general(left, right, (((1,), (1,)), ((), ())), preferred_element_...  17.7 us
    unnamed x1, blocking collectives  16.1 us
    dot_general x1, matrix products, body(): jnp.einsum('qrhd,krhd->rhqk', queries, piece_keys, preferred_element_type...  16 us
    reduce_sum x2, other arithmetic, body(): new_sum = jnp.sum(image_weights, axis=-1) + jnp.sum(text_weights, axis=-1)  15.2 us
  transfers between devices with their start and end apart: 6, of which 4 were waited for; matrix products, arithmetic and copies ran while one was open for 15% of the time, Pallas kernels for 36%

profile of v2, /device:TPU:0, one launch (start us, length us, event | category | flops | bytes accessed | tf_op | source)
XLA Modules:
  0.0 696.8 jit_solution(6084771963052381523)
XLA Ops:
  9.7 100.5 %gather_rows.2 = (bf16[3,2432,768]{2,1,0:T(8,128)(2,1)}, bf16[2,2432,768]{2,1,0:T(8,128)(2,1)}) custom-call(bf16[3,304,768]{2,1,0:T(8,128)(2,1)} %refs_0_.1, bf16[2,304,768]{2,1,0:T(8,128)(2,1)} %refs_1_.1), custom_call_target="tpu_custom_call" | custom-call | bytes 37355520 | tf_op jit(solution)/shard_map/gather_rows/pallas_call | solution.py:219
  111.8 4.6 fusion.57
  132.2 6.7 add.222
  141.8 6.7 mul.301
  148.6 14.7 %fusion.32 = f32[512,3,768]{2,0,1:T(8,128)S(1)} fusion(bf16[3,2432,768]{2,1,0:T(8,128)(2,1)} %get-tuple-element.14, f32[512,2432]{1,0:T(8,128)} %add.222, f32[512,2432]{1,0:T(8,128)} %mul.301, f32[512,2432]{1,0:T(8,128)} %reshape.249, f32[512]{0:T(512)S(1)} %rsqrt.60, f32[512]{0:T(512)S(1)} %div.60), kind=kOutput, calls=%fused_computation.37 | convolution fusion | flops 5744033792 | bytes 30871552 | tf_op jit(solution)/shard_map/rd,kdc->rkc/dot_general | solution.py:274
  168.2 3.4 reduce_sum.119
  181.4 3.4 multiply_reduce_fusion.1
  185.1 254.1 %gather_rows.3 = (bf16[1,2432,768]{2,1,0:T(8,128)(2,1)}, bf16[1,2432,2816]{2,1,0:T(8,128)(2,1)}, bf16[1,2432,2816]{2,1,0:T(8,128)(2,1)}) custom-call(bf16[1,304,768]{2,1,0:T(8,128)(2,1)} %bitcast.156, bf16[1,304,2816]{2,1,0:T(8,128)(2,1)} %bitcast.154, bf16[1,304,2816]{2,1,0:T(8,128)(2,1)} %bitcast.155), custom_call_target="tpu_custom_call" | custom-call | bytes 62259200 | tf_op jit(solution)/shard_map/gather_rows/pallas_call | solution.py:219
  443.7 16.1 %all-reduce = bf16[512]{0:T(512)(128)(2,1)S(1)} all-reduce(bf16[512]{0:T(512)(128)(2,1)S(1)} %dynamic-update-slice), channel_id=1, replica_groups=mesh['cfg'=2,'seq'=8,'wgt'=2] {'seq'}, use_global_device_ids=true, to_apply=%add | all-reduce | flops 512 | bytes 2048
  466.2 6.1 fusion.12
  472.3 10.4 %fusion.77 = (bf16[1024,4,1,768]{0,3,1,2:T(8,128)(2,1)}, bf16[1024,4,1,768]{0,3,1,2:T(8,128)(2,1)}) fusion(bf16[1024,4,2,768]{0,3,1,2:T(8,128)(2,1)} %all-gather.4.cloned.1.call-done), kind=kLoop, calls=%fused_computation.127 | loop fusion | bytes 25165824 | tf_op jit(solution)/shard_map/slice | solution.py:310
  482.8 16.0 %multiply_reduce_fusion = (f32[4,12,128]{2,1,0:T(8,128)S(1)}, f32[4,12,128,1024]{3,2,1,0:T(8,128)}) fusion(bf16[1024,4,12,64]{0,3,2,1:T(8,128)(2,1)} %bitcast.150, bf16[128,4,12,64]{3,2,1,0:T(8,128)(2,1)S(1)} %multiply_convert_fusion), kind=kOutput, calls=%fused_computation.1 | convolution fusion | flops 817883136 | bytes 32268288 | tf_op jit(solution)/shard_map/qrhd,krhd->rhqk/dot_general | solution.py:314
  498.8 11.2 %fusion = f32[4,12,128]{2,1,0:T(8,128)S(1)} fusion(f32[4,12,128,1024]{3,2,1,0:T(8,128)} %get-tuple-element.62, f32[4,12,128]{2,1,0:T(8,128)S(1)} %fusion.69), kind=kLoop, calls=%fused_computation.2 | loop fusion | flops 18868224 | bytes 25214976 | tf_op jit(solution)/shard_map/reduce_sum | solution.py:327
  510.1 4.0 fusion.10
  515.3 12.9 %fusion.37 = bf16[128,4,12,64]{0,3,2,1:T(8,128)(2,1)S(1)} fusion(f32[12,64,4,128]{3,1,0,2:T(8,128)S(1)} %fusion.13, bf16[1024,4,12,64]{0,3,2,1:T(8,128)(2,1)} %bitcast.151, f32[4,12,128,1024]{3,2,1,0:T(8,128)} %get-tuple-element.62, f32[4,12,128]{2,1,0:T(8,128)S(1)} %fusion.69, f32[128,4,12]{0,2,1:T(8,128)S(1)} %fusion.68), kind=kOutput, calls=%fused_computation.51 | convolution fusion | flops 825360384 | bytes 33865728 | tf_op jit(solution)/shard_map/rhqk,krhd->rhqd/dot_general | solution.py:328
  532.4 5.7 convolution_convert_fusion
  545.2 27.5 %reduce-scatter.3.cloned.1.call-done = bf16[256,2432]{1,0:T(8,128)(2,1)} async-done(((bf16[512,2432]{1,0:T(8,128)(2,1)}), bf16[256,2432]{1,0:T(8,128)(2,1)}) %reduce-scatter.3.cloned.1.call-update) | async-done | bytes 1245200 | tf_op jit(solution)/shard_map/reduce_scatter | solution.py:346
  579.6 37.7 %all-gather.8.cloned.1.call-done = bf16[512,2432]{1,0:T(8,128)(2,1)} async-done(((bf16[256,2432]{1,0:T(8,128)(2,1)}), bf16[512,2432]{1,0:T(8,128)(2,1)}) %all-gather.8.cloned.1.call-update) | async-done | bytes 2490384 | tf_op jit(solution)/shard_map/all_gather | solution.py:363
  617.2 12.8 %fusion.22 = bf16[512,2816]{1,0:T(8,128)(2,1)S(1)} fusion(bf16[512,2432]{1,0:T(8,128)(2,1)} %all-gather.8.cloned.1.call-done, bf16[1,2432,2816]{2,1,0:T(8,128)(2,1)} %get-tuple-element.24), kind=kOutput, calls=%fused_computation.26 | convolution fusion | flops 7025852416 | bytes 19070976 | tf_op jit(solution)/shard_map/dot_general | solution.py:366
  630.0 12.0 %fusion.25 = bf16[512,2432]{1,0:T(8,128)(2,1)} fusion(bf16[512,2816]{1,0:T(8,128)(2,1)S(1)} %fusion.22, bf16[1,2432,2816]{2,1,0:T(8,128)(2,1)} %get-tuple-element.25), kind=kOutput, calls=%fused_computation.31 | convolution fusion | flops 7014121472 | bytes 19070976 | tf_op jit(solution)/shard_map/dot_general | solution.py:31
  643.8 3.7 mul.338
  649.3 3.7 add.254
  654.7 3.7 mul.357
  658.4 19.9 %reduce-scatter.5.cloned.1.call-done = bf16[256,2432]{1,0:T(8,128)(2,1)} async-done(((bf16[512,2432]{1,0:T(8,128)(2,1)}), bf16[256,2432]{1,0:T(8,128)(2,1)}) %reduce-scatter.5.cloned.1.call-update) | async-done | bytes 1245200 | tf_op jit(solution)/shard_map/reduce_scatter | solution.py:373
  (143 shorter events, 83.9 us)
Async XLA Ops:
  7.2 676.4 %copy-start = (bf16[2432,64]{0,1:T(8,128)(2,1)S(1)}, bf16[2432,64]{0,1:T(8,128)(2,1)}, u32[]{:S(2)}) copy-start(bf16[2432,64]{0,1:T(8,128)(2,1)} %param.25) | copy-start | bytes 933892
  7.2 104.6 %copy-start.8 = (bf16[1,64,2432]{2,1,0:T(8,128)(2,1)S(1)}, bf16[1,64,2432]{2,1,0:T(8,128)(2,1)}, u32[]{:S(2)}) copy-start(bf16[1,64,2432]{2,1,0:T(8,128)(2,1)} %param.15) | copy-start | bytes 933892
  7.2 103.0 %copy-start.15 = (s32[1,64]{1,0:T(1,128)S(1)}, s32[1,64]{1,0:T(1,128)}, u32[]{:S(2)}) copy-start(s32[1,64]{1,0:T(1,128)} %param.16) | copy-start | bytes 772
  7.2 452.7 %all-gather.6.cloned.1.call-start = ((), (), s32[]{:S(2)}) async-start(), calls=%async_computation.3 | async-start | bytes 1769472 | tf_op jit(solution)/shard_map/all_gather | solution.py:299
  111.8 4.7 copy-start.14
  116.4 6.9 copy-start.1
  121.7 350.7 %all-gather.4.cloned.1.call-start = ((), (), s32[]{:S(2)}) async-start(), calls=%async_computation.2 | async-start | bytes 14155776 | tf_op jit(solution)/shard_map/all_gather | solution.py:298
  177.0 2.0 copy-start.6
  178.3 394.4 %reduce-scatter.3.cloned.1.call-start = ((), (), s32[]{:S(2)}) async-start(), calls=%async_computation.4 | async-start | bytes 3735552 | tf_op jit(solution)/shard_map/reduce_scatter | solution.py:346
  439.3 2.9 copy-start.17
  482.8 27.3 %slice-start = ((s8[12582912]{0:T(1024)(128)(4,1)}), s8[4194304]{0:T(1024)(128)(4,1)S(1)}, s32[]{:S(2)}) async-start(s8[12582912]{0:T(1024)(128)(4,1)} %bitcast.148), calls=%async_computation.7 | async-start | bytes 8388608
  482.8 27.3 %slice-start.1 = ((s8[12582912]{0:T(1024)(128)(4,1)}), s8[4194304]{0:T(1024)(128)(4,1)S(1)}, s32[]{:S(2)}) async-start(s8[12582912]{0:T(1024)(128)(4,1)} %bitcast.148), calls=%async_computation.8 | async-start | bytes 8388608
  498.8 11.3 %slice-start.2 = ((s8[12582912]{0:T(1024)(128)(4,1)}), s8[4194304]{0:T(1024)(128)(4,1)S(1)}, s32[]{:S(2)}) async-start(s8[12582912]{0:T(1024)(128)(4,1)} %bitcast.148), calls=%async_computation.9 | async-start | bytes 8388608
  510.1 4.0 copy-start.7
  532.4 5.8 copy-start.12
  538.2 79.0 %all-gather.8.cloned.1.call-start = ((), (), s32[]{:S(2)}) async-start(), calls=%async_computation.5 | async-start | bytes 3735552 | tf_op jit(solution)/shard_map/all_gather | solution.py:363
  540.9 2.0 copy-start.10
  572.7 3.8 copy-start.5
  579.5 98.8 %reduce-scatter.5.cloned.1.call-start = ((), (), s32[]{:S(2)}) async-start(), calls=%async_computation.6 | async-start | bytes 3735552 | tf_op jit(solution)/shard_map/reduce_scatter | solution.py:373
  630.0 12.0 %copy-start.9 = (f32[4,2432]{1,0:T(4,128)S(1)}, f32[4,2432]{1,0:T(4,128)}, u32[]{:S(2)}) copy-start(f32[4,2432]{1,0:T(4,128)} %get-tuple-element.55) | copy-start | bytes 116740
  678.3 3.0 copy-start.3
  683.2 2.4 copy-start.16
  683.2 5.2 copy-start.13
  684.1 4.3 collective-permute-start
  (3 other events, 5.5 us)
Sparse Core Ops, SparseCore 0:
  121.8 24.2 all-gather.5
  178.4 184.7 all-gather.3
  538.3 34.3 reduce-scatter.2
  579.6 37.5 all-gather.7
  642.1 36.1 reduce-scatter.4

commit v3 on v2

--- a/solution.py
+++ b/solution.py
@@ -360,9 +360,19 @@
     branch_in = (layer_norm(residual) * (1.0 + modulate[:, 6]) + modulate[:, 5]).astype(
         jnp.bfloat16
     )
-    branch_rows = lax.all_gather(
-        branch_in.reshape(share_rows, feat_width), "wgt", axis=0, tiled=True
-    )
+    own_rows = branch_in.reshape(share_rows, feat_width)
+    if lax.axis_size("wgt") == 2:
+        other_rows = from_partner(own_rows, "wgt", 0)
+        is_low = lax.axis_index("wgt") == 0
+        branch_rows = jnp.concatenate(
+            [
+                jnp.where(is_low, own_rows, other_rows),
+                jnp.where(is_low, other_rows, own_rows),
+            ],
+            axis=0,
+        )
+    else:
+        branch_rows = lax.all_gather(own_rows, "wgt", axis=0, tiled=True)
     expanded = jnp.dot(
         branch_rows,
         expand_full[0],

time: 703 us -> 698 us (level)
  waiting for transfers between devices: 87.8 us -> 77.9 us
    all_gather x1 -> x0, waiting for transfers between devices: 37.7 us -> none  [body(): lax.all_gather(branch_in.reshape(share_rows, feat_width), 'wgt', axis=0,...]
    ppermute x1 -> x2, waiting for transfers between devices: 2.7 us -> 31.8 us  [from_partner(): return lax.ppermute(value, axis, pairs)]
    dot_general x1 -> x0, matrix products: 12.8 us -> none  [body(): jnp.dot(branch_rows, expand_full[0], preferred_element_type=jnp.float32)]
    dot_general x2, matrix products: 17.7 us -> 30 us  [rows_by_rows(): lax.dot_general(left, right, (((1,), (1,)), ((), ())), preferred_element_...]
  transfers between devices with their start and end apart: 6 -> 6, of which waited for: 4 -> 4; matrix products, arithmetic and copies ran while one was open for 15% -> 15% of each run, Pallas kernels for 36% -> 37%
where the time goes in v3:
time: 698 us; the launch traced here: 691 us
  Pallas kernels  355 us (51%)
  matrix products  87.5 us (13%)
  local copies, waits for them, and re-layouts  87.4 us (13%)
  waiting for transfers between devices  77.9 us (11%)
  other arithmetic  50.1 us (7%)
  blocking collectives  16.3 us (2%)
  between operations  15.2 us (2%)
    pallas_call x2, Pallas kernels, gather_rows(): pl.pallas_call(lambda *refs: gather_kernel(count, seq_size, *refs), out_s...  355 us
    ppermute x2, waiting for transfers between devices, from_partner(): return lax.ppermute(value, axis, pairs)  31.8 us
    dot_general x2, matrix products, rows_by_rows(): lax.dot_general(left, right, (((1,), (1,)), ((), ())), preferred_element_...  30 us
    reduce_scatter x1, waiting for transfers between devices, body(): lax.psum_scatter(rows_by_rows(piece_rows, out_full[0]).astype(jnp.bfloat1...  26.9 us
    reduce_scatter x1, waiting for transfers between devices, body(): lax.psum_scatter(rows_by_rows(piece_rows, contract_full[0]).astype(jnp.bf...  19.1 us
    unnamed x1, blocking collectives  16.3 us
    dot_general x1, matrix products, body(): jnp.einsum('qrhd,krhd->rhqk', queries, piece_keys, preferred_element_type...  16.1 us
    reduce_sum x2, other arithmetic, body(): new_sum = jnp.sum(image_weights, axis=-1) + jnp.sum(text_weights, axis=-1)  15.2 us
  transfers between devices with their start and end apart: 6, of which 4 were waited for; matrix products, arithmetic and copies ran while one was open for 15% of the time, Pallas kernels for 37%

profile of v3, /device:TPU:0, one launch (start us, length us, event | category | flops | bytes accessed | tf_op | source)
XLA Modules:
  0.0 691.1 jit_solution(13424467783047352771)
XLA Ops:
  9.7 100.5 %gather_rows.2 = (bf16[3,2432,768]{2,1,0:T(8,128)(2,1)}, bf16[2,2432,768]{2,1,0:T(8,128)(2,1)}) custom-call(bf16[3,304,768]{2,1,0:T(8,128)(2,1)} %refs_0_.1, bf16[2,304,768]{2,1,0:T(8,128)(2,1)} %refs_1_.1), custom_call_target="tpu_custom_call" | custom-call | bytes 37355520 | tf_op jit(solution)/shard_map/gather_rows/pallas_call | solution.py:219
  111.8 4.6 fusion.64
  131.9 6.7 add.222
  141.5 6.7 mul.301
  148.3 14.7 %fusion.32 = f32[512,3,768]{2,0,1:T(8,128)S(1)} fusion(bf16[3,2432,768]{2,1,0:T(8,128)(2,1)} %get-tuple-element.14, f32[512,2432]{1,0:T(8,128)} %add.222, f32[512,2432]{1,0:T(8,128)} %mul.301, f32[512,2432]{1,0:T(8,128)} %reshape.249, f32[512]{0:T(512)S(1)} %rsqrt.60, f32[512]{0:T(512)S(1)} %div.60), kind=kOutput, calls=%fused_computation.37 | convolution fusion | flops 5744033792 | bytes 30871552 | tf_op jit(solution)/shard_map/rd,kdc->rkc/dot_general | solution.py:274
  167.9 3.4 reduce_sum.119
  181.1 3.4 multiply_reduce_fusion.1
  184.8 254.2 %gather_rows.3 = (bf16[1,2432,768]{2,1,0:T(8,128)(2,1)}, bf16[1,2432,2816]{2,1,0:T(8,128)(2,1)}, bf16[1,2432,2816]{2,1,0:T(8,128)(2,1)}) custom-call(bf16[1,304,768]{2,1,0:T(8,128)(2,1)} %bitcast.156, bf16[1,304,2816]{2,1,0:T(8,128)(2,1)} %bitcast.154, bf16[1,304,2816]{2,1,0:T(8,128)(2,1)} %bitcast.155), custom_call_target="tpu_custom_call" | custom-call | bytes 62259200 | tf_op jit(solution)/shard_map/gather_rows/pallas_call | solution.py:219
  443.4 16.3 %all-reduce = bf16[512]{0:T(512)(128)(2,1)S(1)} all-reduce(bf16[512]{0:T(512)(128)(2,1)S(1)} %dynamic-update-slice), channel_id=1, replica_groups=mesh['cfg'=2,'seq'=8,'wgt'=2] {'seq'}, use_global_device_ids=true, to_apply=%add | all-reduce | flops 512 | bytes 2048
  466.2 6.1 fusion.12
  472.3 10.4 %fusion.90 = (bf16[1024,4,1,768]{0,3,1,2:T(8,128)(2,1)}, bf16[1024,4,1,768]{0,3,1,2:T(8,128)(2,1)}) fusion(bf16[1024,4,2,768]{0,3,1,2:T(8,128)(2,1)} %all-gather.3.cloned.1.call-done), kind=kLoop, calls=%fused_computation.137 | loop fusion | bytes 25165824 | tf_op jit(solution)/shard_map/slice | solution.py:310
  482.7 16.1 %multiply_reduce_fusion = (f32[4,12,128]{2,1,0:T(8,128)S(1)}, f32[4,12,128,1024]{3,2,1,0:T(8,128)}) fusion(bf16[1024,4,12,64]{0,3,2,1:T(8,128)(2,1)} %bitcast.150, bf16[128,4,12,64]{3,2,1,0:T(8,128)(2,1)S(1)} %multiply_convert_fusion), kind=kOutput, calls=%fused_computation.1 | convolution fusion | flops 817883136 | bytes 32268288 | tf_op jit(solution)/shard_map/qrhd,krhd->rhqk/dot_general | solution.py:314
  498.8 11.2 %fusion = f32[4,12,128]{2,1,0:T(8,128)S(1)} fusion(f32[4,12,128,1024]{3,2,1,0:T(8,128)} %get-tuple-element.64, f32[4,12,128]{2,1,0:T(8,128)S(1)} %fusion.76), kind=kLoop, calls=%fused_computation.2 | loop fusion | flops 18868224 | bytes 25214976 | tf_op jit(solution)/shard_map/reduce_sum | solution.py:327
  510.1 4.0 fusion.10
  515.3 12.8 %fusion.40 = bf16[128,4,12,64]{0,3,2,1:T(8,128)(2,1)S(1)} fusion(f32[12,64,4,128]{3,1,0,2:T(8,128)S(1)} %fusion.13, bf16[1024,4,12,64]{0,3,2,1:T(8,128)(2,1)} %bitcast.151, f32[4,12,128,1024]{3,2,1,0:T(8,128)} %get-tuple-element.64, f32[4,12,128]{2,1,0:T(8,128)S(1)} %fusion.76, f32[128,4,12]{0,2,1:T(8,128)S(1)} %fusion.75), kind=kOutput, calls=%fused_computation.54 | convolution fusion | flops 825360384 | bytes 33865728 | tf_op jit(solution)/shard_map/rhqk,krhd->rhqd/dot_general | solution.py:328
  532.4 5.7 convolution_convert_fusion
  545.8 26.9 %reduce-scatter.3.cloned.1.call-done = bf16[256,2432]{1,0:T(8,128)(2,1)} async-done(((bf16[512,2432]{1,0:T(8,128)(2,1)}), bf16[256,2432]{1,0:T(8,128)(2,1)}) %reduce-scatter.3.cloned.1.call-update) | async-done | bytes 1245200 | tf_op jit(solution)/shard_map/reduce_scatter | solution.py:346
  572.6 3.4 fusion.89
  579.7 29.1 %collective-permute-done = bf16[256,2432]{1,0:T(8,128)(2,1)} collective-permute-done((bf16[256,2432]{1,0:T(8,128)(2,1)}, bf16[256,2432]{1,0:T(8,128)(2,1)}, u32[]{:S(2)}, u32[]{:S(2)}) %collective-permute-start) | collective-permute-done | bytes 1245216 | tf_op jit(solution)/shard_map/ppermute | solution.py:20
  612.2 24.3 %fusion.25 = bf16[512,2432]{1,0:T(8,128)(2,1)} fusion(bf16[1,2432,2816]{2,1,0:T(8,128)(2,1)} %get-tuple-element.25, bf16[1,2432,2816]{2,1,0:T(8,128)(2,1)} %get-tuple-element.24, bf16[256,2432]{1,0:T(8,128)(2,1)} %get-tuple-element.50, bf16[256,2432]{1,0:T(8,128)(2,1)} %get-tuple-element.49), kind=kOutput, calls=%fused_computation.31 | convolution fusion | flops 14044954624 | bytes 32374784 | tf_op jit(solution)/shard_map/dot_general | solution.py:31
  639.0 3.7 mul.338
  644.6 3.7 add.254
  650.0 3.7 mul.357
  653.7 19.1 %reduce-scatter.5.cloned.1.call-done = bf16[256,2432]{1,0:T(8,128)(2,1)} async-done(((bf16[512,2432]{1,0:T(8,128)(2,1)}), bf16[256,2432]{1,0:T(8,128)(2,1)}) %reduce-scatter.5.cloned.1.call-update) | async-done | bytes 1245200 | tf_op jit(solution)/shard_map/reduce_scatter | solution.py:383
  (142 shorter events, 85.3 us)
Async XLA Ops:
  7.2 670.9 %copy-start = (bf16[2432,64]{0,1:T(8,128)(2,1)S(1)}, bf16[2432,64]{0,1:T(8,128)(2,1)}, u32[]{:S(2)}) copy-start(bf16[2432,64]{0,1:T(8,128)(2,1)} %param.25) | copy-start | bytes 933892
  7.2 104.6 %copy-start.8 = (bf16[1,64,2432]{2,1,0:T(8,128)(2,1)S(1)}, bf16[1,64,2432]{2,1,0:T(8,128)(2,1)}, u32[]{:S(2)}) copy-start(bf16[1,64,2432]{2,1,0:T(8,128)(2,1)} %param.15) | copy-start | bytes 933892
  7.2 103.0 %copy-start.15 = (s32[1,64]{1,0:T(1,128)S(1)}, s32[1,64]{1,0:T(1,128)}, u32[]{:S(2)}) copy-start(s32[1,64]{1,0:T(1,128)} %param.16) | copy-start | bytes 772
  7.2 452.6 %all-gather.5.cloned.1.call-start = ((), (), s32[]{:S(2)}) async-start(), calls=%async_computation.3 | async-start | bytes 1769472 | tf_op jit(solution)/shard_map/all_gather | solution.py:299
  111.8 4.7 copy-start.14
  116.4 6.9 copy-start.1
  121.7 350.6 %all-gather.3.cloned.1.call-start = ((), (), s32[]{:S(2)}) async-start(), calls=%async_computation.2 | async-start | bytes 14155776 | tf_op jit(solution)/shard_map/all_gather | solution.py:298
  176.7 2.0 copy-start.6
  178.0 394.6 %reduce-scatter.3.cloned.1.call-start = ((), (), s32[]{:S(2)}) async-start(), calls=%async_computation.4 | async-start | bytes 3735552 | tf_op jit(solution)/shard_map/reduce_scatter | solution.py:346
  439.0 2.9 copy-start.17
  482.7 27.3 %slice-start = ((s8[12582912]{0:T(1024)(128)(4,1)}), s8[4194304]{0:T(1024)(128)(4,1)S(1)}, s32[]{:S(2)}) async-start(s8[12582912]{0:T(1024)(128)(4,1)} %bitcast.148), calls=%async_computation.6 | async-start | bytes 8388608
  482.7 27.3 %slice-start.1 = ((s8[12582912]{0:T(1024)(128)(4,1)}), s8[4194304]{0:T(1024)(128)(4,1)S(1)}, s32[]{:S(2)}) async-start(s8[12582912]{0:T(1024)(128)(4,1)} %bitcast.148), calls=%async_computation.7 | async-start | bytes 8388608
  498.8 11.3 %slice-start.2 = ((s8[12582912]{0:T(1024)(128)(4,1)}), s8[4194304]{0:T(1024)(128)(4,1)S(1)}, s32[]{:S(2)}) async-start(s8[12582912]{0:T(1024)(128)(4,1)} %bitcast.148), calls=%async_computation.8 | async-start | bytes 8388608
  510.1 4.0 copy-start.7
  538.1 134.6 %reduce-scatter.5.cloned.1.call-start = ((), (), s32[]{:S(2)}) async-start(), calls=%async_computation.5 | async-start | bytes 3735552 | tf_op jit(solution)/shard_map/reduce_scatter | solution.py:383
  539.2 2.0 copy-start.11
  541.5 2.0 copy-start.10
  572.6 3.8 copy-start.5
  579.4 29.4 %collective-permute-start = (bf16[256,2432]{1,0:T(8,128)(2,1)}, bf16[256,2432]{1,0:T(8,128)(2,1)}, u32[]{:S(2)}, u32[]{:S(2)}) collective-permute-start(bf16[256,2432]{1,0:T(8,128)(2,1)} %add_convert_fusion.2), channel_id=1, source_target_pairs={{0,1},{1,0},{2,3},{3,2},{4,5},{5,4},{6,7},{7,6},{8,9},{9,8},{10,11... | collective-permute-start | bytes 3735560 | tf_op jit(solution)/shard_map/ppermute | solution.py:20
  672.8 3.0 copy-start.3
  675.4 1.8 copy-start.2
  677.7 2.4 copy-start.16
  677.7 5.2 copy-start.13
  678.6 4.3 collective-permute-start.1
  (3 other events, 3.3 us)
Sparse Core Ops, SparseCore 0:
  121.8 24.2 all-gather.4
  178.1 184.7 all-gather.2
  538.3 34.3 reduce-scatter.2
  636.6 36.1 reduce-scatter.4
